TPU v7x, 32 devices: a whole 2x2x4 slice. The times are simulated.
32 devices in a mesh: blk: 32 (over z, y, x, core), grp: 1.
Axes of the slice: x: 2, y: 2, z: 4, core: 2. Of those that a mesh axis runs over, the one named last changes fastest.
Arguments:
- fields: float32 [3, 768, 32, 256], P(None, 'blk', 'grp'), may hold values from -100 to 100
- mask: int32 [32, 256], P('grp'), may hold values from 0 to 1, as said below
Outputs:
- r_factor: float32 [768, 768], replicated
- active_force: float32 [2, 768, 32, 256], P(None, 'blk', 'grp')
Inputs may be any that keep to these rules, and one draw needn't show every extreme that they name: `mask`: grid rows k * 32 to (k + 1) * 32 - 1, for each k, hold exactly 4352 fluid points together.
All inputs are finite; a program needn't handle non-finite values.
Results may differ from a plain program's by a relative error of at most 0.0003.
Values sent between devices are 32-bit elements; how exact they have to be, the bound alone decides.
A program may use at most 256 MiB of HBM per device.

v0:
```python
import jax
import jax.numpy as jnp
from jax import lax
from jax.sharding import PartitionSpec as P


def padded(cells, sides, width):
    for axis, dim in sides:
        count = lax.axis_size(axis)
        head = lax.slice_in_dim(cells, 0, width, axis=dim)
        tail = lax.slice_in_dim(cells, cells.shape[dim] - width, cells.shape[dim], axis=dim)
        cells = jnp.concatenate(
            [
                lax.ppermute(tail, axis, [(i, (i + 1) % count) for i in range(count)]),
                cells,
                lax.ppermute(head, axis, [((i + 1) % count, i) for i in range(count)]),
            ],
            axis=dim,
        )
    return cells


def pair_gram(left_block, right_block):
    return jnp.einsum("ftm,fsm->ts", left_block, right_block, precision=lax.Precision.HIGHEST)


def per_device(fields, mask):
    widened = padded(fields[1:3], (("grp", 2),), 1)
    middle = widened[:, :, 1:-1]
    slope_rows = 0.5 * (widened[:, :, 2:] - widened[:, :, :-2])
    slope_cols = 0.5 * (jnp.roll(middle, -1, 3) - jnp.roll(middle, 1, 3))
    active_force = jnp.stack([slope_rows[0] + slope_cols[1], slope_rows[1] - slope_cols[0]])
    stacked = jnp.concatenate([fields, active_force], 0)
    groups = lax.axis_size("grp")
    rows_here, columns = mask.shape
    weighted = stacked * mask.astype(jnp.float32)[None, None]
    relaid = lax.all_to_all(weighted, "blk", split_axis=2, concat_axis=1, tiled=True)
    snapshots = relaid.reshape(relaid.shape[0], relaid.shape[1], -1)
    gram_matrix = lax.psum(pair_gram(snapshots, snapshots), ("blk", "grp"))
    gram_matrix = gram_matrix / float(rows_here * groups * columns)
    r_factor = jnp.linalg.cholesky(gram_matrix).T
    return (r_factor, active_force)


def solution(mesh):
    placed = (P(None, "blk", "grp", None), P("grp", None))
    return jax.shard_map(
        per_device,
        mesh=mesh,
        in_specs=placed,
        out_specs=(P(), P(None, "blk", "grp", None)),
        check_vma=False,
    )
```

profile of v0, /device:TPU:0, one launch (start us, length us, event | category | flops | bytes accessed | tf_op | source)
XLA Modules:
  0.0 414.7 jit_solution(1925063667239120276)
XLA Ops:
  7.2 3.0 copy.15
  14.2 95.6 %all_to_all.15 = f32[5,24,32,256]{3,1,0,2:T(8,128)S(1)} all-to-all(f32[5,24,32,256]{3,1,0,2:T(8,128)S(1)} %maximum_multiply_fusion), channel_id=1, replica_groups=mesh['blk'=32,'grp'=1] {'blk'}, dimensions={2} | all-to-all | bytes 7864320 | tf_op jit(solution)/shard_map/all_to_all | solution.py:37
  110.2 10.9 %convolution_bitcast_fusion = f32[768,768]{0,1:T(8,128)} fusion(f32[5,768,256]{2,1,0:T(8,128)S(1)} %bitcast.43), kind=kOutput, calls=%fused_computation.5 | convolution fusion | flops 9059696640 | bytes 6291456 | tf_op jit(solution)/shard_map/ftm,fsm->ts/dot_general | solution.py:24
  122.4 2.1 copy.20
  124.4 131.0 %all-reduce.3.cloned.1.call-done = f32[768,768]{0,1:T(8,128)} async-done(((f32[768,768]{0,1:T(8,128)}), f32[768,768]{0,1:T(8,128)}) %all-reduce.3.cloned.1.call-update) | async-done | bytes 2359312 | tf_op jit(solution)/shard_map/psum | solution.py:39
  255.5 3.2 broadcast_multiply_fusion
  258.7 3.3 copy.18
  262.1 2.0 fusion
  265.4 11.7 %cholesky.165 = f32[128,128]{1,0:T(8,128)S(1)} custom-call(f32[128,128]{1,0:T(8,128)S(1)} %cholesky.424), custom_call_target="Cholesky" | custom-call | tf_op jit(solution)/shard_map/jit(cholesky)/cholesky | solution.py:41
  277.3 9.8 %custom-call.43 = f32[1,128,128]{1,2,0:T(8,128)S(1)} custom-call(f32[1,128,128]{2,1,0:T(8,128)S(1)} %get-tuple-element.29), custom_call_target="InvertDiagBlocksLowerTriangular" | custom-call | tf_op jit(solution)/shard_map/jit(cholesky)/cholesky | solution.py:41
  290.0 11.7 %cholesky.188 = f32[128,128]{1,0:T(8,128)S(1)} custom-call(f32[128,128]{1,0:T(8,128)S(1)} %cholesky.428), custom_call_target="Cholesky" | custom-call | tf_op jit(solution)/shard_map/jit(cholesky)/cholesky | solution.py:41
  301.7 10.0 %custom-call.44 = f32[1,128,128]{1,2,0:T(8,128)S(1)} custom-call(f32[1,128,128]{2,1,0:T(8,128)S(1)} %get-tuple-element.26), custom_call_target="InvertDiagBlocksLowerTriangular" | custom-call | tf_op jit(solution)/shard_map/jit(cholesky)/cholesky | solution.py:41
  312.1 1.5 convolution_subtract_fusion.1
  313.7 11.7 %cholesky.354 = f32[128,128]{1,0:T(8,128)S(1)} custom-call(f32[128,128]{1,0:T(8,128)S(1)} %cholesky.433), custom_call_target="Cholesky" | custom-call | tf_op jit(solution)/shard_map/jit(cholesky)/cholesky | solution.py:41
  326.1 9.8 %custom-call.45 = f32[1,128,128]{1,2,0:T(8,128)S(1)} custom-call(f32[1,128,128]{2,1,0:T(8,128)S(1)} %get-tuple-element.23), custom_call_target="InvertDiagBlocksLowerTriangular" | custom-call | tf_op jit(solution)/shard_map/jit(cholesky)/cholesky | solution.py:41
  336.3 1.6 convolution_subtract_fusion.2
  337.8 12.1 %cholesky.373 = f32[128,128]{1,0:T(8,128)S(1)} custom-call(f32[128,128]{1,0:T(8,128)S(1)} %cholesky.438), custom_call_target="Cholesky" | custom-call | tf_op jit(solution)/shard_map/jit(cholesky)/cholesky | solution.py:41
  350.6 9.8 %custom-call.46 = f32[1,128,128]{1,2,0:T(8,128)S(1)} custom-call(f32[1,128,128]{2,1,0:T(8,128)S(1)} %get-tuple-element.20), custom_call_target="InvertDiagBlocksLowerTriangular" | custom-call | tf_op jit(solution)/shard_map/jit(cholesky)/cholesky | solution.py:41
  360.7 1.5 convolution_subtract_fusion.3
  362.2 11.7 %cholesky.392 = f32[128,128]{1,0:T(8,128)S(1)} custom-call(f32[128,128]{1,0:T(8,128)S(1)} %cholesky.443), custom_call_target="Cholesky" | custom-call | tf_op jit(solution)/shard_map/jit(cholesky)/cholesky | solution.py:41
  374.6 9.8 %custom-call.47 = f32[1,128,128]{1,2,0:T(8,128)S(1)} custom-call(f32[1,128,128]{2,1,0:T(8,128)S(1)} %get-tuple-element.17), custom_call_target="InvertDiagBlocksLowerTriangular" | custom-call | tf_op jit(solution)/shard_map/jit(cholesky)/cholesky | solution.py:41
  385.9 11.9 %cholesky.410 = f32[128,128]{1,0:T(8,128)S(1)} custom-call(f32[128,128]{1,0:T(8,128)S(1)} %convolution_subtract_fusion.4), custom_call_target="Cholesky" | custom-call | tf_op jit(solution)/shard_map/jit(cholesky)/cholesky | solution.py:41
  403.0 1.6 select_bitcast_fusion
  404.6 3.0 copy.19
  (51 shorter events, 15.9 us)
Async XLA Ops:
  7.2 248.3 %all-reduce.3.cloned.1.call-start = ((), (), s32[]{:S(2)}) async-start(), calls=%async_computation.1 | async-start | bytes 4718592 | tf_op jit(solution)/shard_map/psum | solution.py:39
  10.3 2.3 collective-permute-start
  10.3 2.3 collective-permute-start.1
  11.8 0.8 copy-start.4
  13.0 0.9 copy-start.1
  121.1 1.1 copy-start.2
  258.7 3.3 copy-start
  264.0 1.4 copy-start.3
Sparse Core Ops, SparseCore 0:
  121.3 134.1 all-reduce.2
where the time goes:
time: 419 us; the launch traced here: 415 us
  other arithmetic  132 us (32%)
  waiting for transfers between devices  131 us (31%)
  blocking collectives  95.6 us (23%)
  matrix products  20.8 us (5%)
  between operations  18.3 us (4%)
  local copies, waits for them, and re-layouts  17 us (4%)
    psum x1, waiting for transfers between devices, per_device(): gram_matrix = lax.psum(pair_gram(snapshots, snapshots), ('blk', 'grp'))  131 us
    another operation x22, other arithmetic, per_device(): r_factor = jnp.linalg.cholesky(gram_matrix).T  124 us
    all_to_all x1, blocking collectives, per_device(): lax.all_to_all(weighted, 'blk', split_axis=2, concat_axis=1, tiled=True)  95.6 us
    unnamed x13, local copies, waits for them, and re-layouts  12.1 us
    dot_general x1, matrix products, pair_gram(): jnp.einsum('ftm,fsm->ts', left_block, right_block, precision=lax.Precisio...  10.9 us
    another operation x10, matrix products, per_device(): r_factor = jnp.linalg.cholesky(gram_matrix).T  9.81 us
  transfers between devices with their start and end apart: 3, of which 1 were waited for; matrix products, arithmetic and copies ran while one was open for 1% of the time, Pallas kernels for 0%

commit v1 on v0

--- a/solution.py
+++ b/solution.py
@@ -1,7 +1,189 @@
+import functools
 import jax
 import jax.numpy as jnp
 from jax import lax
+from jax.experimental import pallas as pl
+from jax.experimental.pallas import tpu as pltpu
 from jax.sharding import PartitionSpec as P
+
+NB = 128
+HIGHEST = lax.Precision.HIGHEST
+MESH_ID = pl.DeviceIdType.MESH
+
+
+def tiles(size):
+    n = size // NB
+    return [(i, j) for i in range(n) for j in range(i, n)]
+
+
+def packed_rows(size, count):
+    unit = 8 * count
+    return -(-len(tiles(size)) * NB // unit) * unit
+
+
+def stages(count):
+    return [(1, 2), (2, 4), (8, count // 8)]
+
+
+def sum_kernel(count, g_ref, full, acc, buf0, buf1, buf2, send, recv, gsend, grecv):
+    me = lax.axis_index("blk")
+    plan = stages(count)
+    bufs = [buf0, buf1, buf2]
+
+    def peer(stride, size, step):
+        here = (me // stride) % size
+        there = (here + step) % size
+        return there, me + (there - here) * stride
+
+    barrier = pltpu.get_barrier_semaphore()
+    greeted = 0
+    for stride, size in plan:
+        for step in range(1, size):
+            pl.semaphore_signal(barrier, inc=1, device_id={"blk": peer(stride, size, step)[1]}, device_id_type=MESH_ID)
+            greeted += 1
+    for b, (i, j) in enumerate(tiles(g_ref.shape[0])):
+        acc[b * NB:(b + 1) * NB, :] = g_ref[i * NB:(i + 1) * NB, j * NB:(j + 1) * NB]
+    used = len(tiles(g_ref.shape[0])) * NB
+    total = acc.shape[0]
+    if used < total:
+        acc[used:, :] = jnp.zeros((total - used, NB), jnp.float32)
+    pl.semaphore_wait(barrier, greeted)
+
+    started = []
+    base = 0
+    length = total
+    slot = 0
+    owned = []
+    for (stride, size), buf in zip(plan, bufs):
+        length = length // size
+        here = (me // stride) % size
+        wave = []
+        for step in range(1, size):
+            there, device = peer(stride, size, step)
+            copy = pltpu.make_async_remote_copy(
+                src_ref=acc.at[pl.ds(pl.multiple_of(base + there * length, 8), length)],
+                dst_ref=buf.at[step - 1],
+                send_sem=send.at[slot], recv_sem=recv.at[slot],
+                device_id={"blk": device}, device_id_type=MESH_ID)
+            copy.start()
+            wave.append(copy)
+            slot += 1
+        base = pl.multiple_of(base + here * length, 8)
+        value = acc[pl.ds(base, length), :]
+        for step, copy in enumerate(wave):
+            copy.wait_recv()
+            value = value + buf[step]
+        acc[pl.ds(base, length), :] = value
+        owned.append((base, length))
+        started += wave
+    full[pl.ds(base, length), :] = acc[pl.ds(base, length), :]
+    slot = 0
+    for (stride, size), (base, length) in reversed(list(zip(plan, owned))):
+        piece = pl.ds(base, length)
+        wave = []
+        for step in range(1, size):
+            copy = pltpu.make_async_remote_copy(
+                src_ref=full.at[piece], dst_ref=full.at[piece],
+                send_sem=gsend.at[slot], recv_sem=grecv.at[slot],
+                device_id={"blk": peer(stride, size, step)[1]}, device_id_type=MESH_ID)
+            copy.start()
+            wave.append(copy)
+            slot += 1
+        for copy in wave:
+            copy.wait_recv()
+        started += wave
+    for copy in started:
+        copy.wait_send()
+
+
+def summed(gram):
+    count = lax.axis_size("blk")
+    size = gram.shape[0]
+    total = packed_rows(size, count)
+    plan = stages(count)
+    lengths = [total // 2, total // 8, total // count]
+    copies = sum(s - 1 for _, s in plan)
+    return pl.pallas_call(
+        functools.partial(sum_kernel, count),
+        out_shape=jax.ShapeDtypeStruct((total, NB), jnp.float32),
+        in_specs=[pl.BlockSpec(memory_space=pltpu.VMEM)],
+        out_specs=pl.BlockSpec(memory_space=pltpu.VMEM),
+        scratch_shapes=[pltpu.VMEM((total, NB), jnp.float32)]
+        + [pltpu.VMEM((s - 1, rows, NB), jnp.float32) for (_, s), rows in zip(plan, lengths)]
+        + [pltpu.SemaphoreType.DMA((copies,))] * 4,
+        compiler_params=pltpu.CompilerParams(collective_id=0, has_side_effects=True, vmem_limit_bytes=56 * 2**20),
+    )(gram)
+
+
+def factor(work, j, u_ref, z_ref):
+    base = pl.multiple_of(j * NB, NB)
+    D = [work[pl.ds(base + 8 * i, 8), pl.ds(base, NB)] for i in range(16)]
+    rows = lax.broadcasted_iota(jnp.int32, (8, NB), 0)
+    lanes = lax.broadcasted_iota(jnp.int32, (8, NB), 1)
+    Z = [jnp.where(rows + 8 * i == lanes, 1.0, 0.0).astype(jnp.float32) for i in range(16)]
+    full = lambda x: jnp.broadcast_to(x, (8, NB))
+    for t in range(16):
+        C = [full(D[t][:, 8 * t + c:8 * t + c + 1]) for c in range(8)]
+        X, Y = D[t], Z[t]
+        for s in range(8):
+            piv = full(C[s][s:s + 1])
+            rs = lax.rsqrt(piv)
+            xr, yr = full(X[s:s + 1]) * rs, full(Y[s:s + 1]) * rs
+            u_ref[8 * t + s:8 * t + s + 1, :] = xr[s:s + 1]
+            z_ref[8 * t + s:8 * t + s + 1, :] = yr[s:s + 1]
+            inv = rs * rs
+            mult = C[s] * inv
+            X0, Y0 = full(X[s:s + 1]), full(Y[s:s + 1])
+            X = jnp.where(rows == s, X0 * inv, X - mult * X0)
+            Y = jnp.where(rows == s, Y0 * inv, Y - mult * Y0)
+            for c in range(s + 1, 8):
+                c0 = full(C[c][s:s + 1])
+                C[c] = jnp.where(rows == s, c0 * inv, C[c] - mult * c0)
+        for i in range(t + 1, 16):
+            d, z = D[i], Z[i]
+            cols = [full(D[i][:, 8 * t + c:8 * t + c + 1]) for c in range(8)]
+            for c in range(8):
+                d = d - cols[c] * full(X[c:c + 1])
+                z = z - cols[c] * full(Y[c:c + 1])
+            D[i], Z[i] = d, z
+
+
+def chol_kernel(scale, g_ref, r_ref, work, u_ref, z_ref):
+    size = work.shape[0]
+    n = size // NB
+    for b, (i, j) in enumerate(tiles(size)):
+        work[i * NB:(i + 1) * NB, j * NB:(j + 1) * NB] = g_ref[b * NB:(b + 1) * NB, :] * scale
+    for i in range(1, n):
+        r_ref[i * NB:(i + 1) * NB, :i * NB] = jnp.zeros((NB, i * NB), jnp.float32)
+    tri = lax.broadcasted_iota(jnp.int32, (NB, NB), 0) <= lax.broadcasted_iota(jnp.int32, (NB, NB), 1)
+
+    @pl.loop(0, n)
+    def _(j):
+        factor(work, j, u_ref, z_ref)
+        for jj in range(n):
+            @pl.when(j == jj)
+            def _(jj=jj):
+                lo, hi = jj * NB, (jj + 1) * NB
+                r_ref[lo:hi, lo:hi] = jnp.where(tri, u_ref[...], 0.0)
+                if jj < n - 1:
+                    panel = jnp.dot(z_ref[...], work[lo:hi, hi:], precision=HIGHEST, preferred_element_type=jnp.float32)
+                    r_ref[lo:hi, hi:] = panel
+                    step = 2 * NB
+                    for a in range(hi, size, step):
+                        b = min(a + step, size)
+                        strip = lax.dot_general(r_ref[lo:hi, a:b], r_ref[lo:hi, a:], (((0,), (0,)), ((), ())), precision=HIGHEST, preferred_element_type=jnp.float32)
+                        work[a:b, a:] = work[a:b, a:] - strip
+
+
+def factored(packed, size, scale):
+    return pl.pallas_call(
+        functools.partial(chol_kernel, scale),
+        out_shape=jax.ShapeDtypeStruct((size, size), jnp.float32),
+        in_specs=[pl.BlockSpec(memory_space=pltpu.VMEM)],
+        out_specs=pl.BlockSpec(memory_space=pltpu.VMEM),
+        scratch_shapes=[pltpu.VMEM((size, size), jnp.float32), pltpu.VMEM((NB, NB), jnp.float32), pltpu.VMEM((NB, NB), jnp.float32)],
+        compiler_params=pltpu.CompilerParams(vmem_limit_bytes=56 * 2**20),
+    )(packed)
 
 
 def padded(cells, sides, width):
@@ -21,7 +203,7 @@
 
 
 def pair_gram(left_block, right_block):
-    return jnp.einsum("ftm,fsm->ts", left_block, right_block, precision=lax.Precision.HIGHEST)
+    return jnp.einsum("ftm,fsm->ts", left_block, right_block, precision=lax.Precision.HIGH)
 
 
 def per_device(fields, mask):
@@ -36,9 +218,10 @@
     weighted = stacked * mask.astype(jnp.float32)[None, None]
     relaid = lax.all_to_all(weighted, "blk", split_axis=2, concat_axis=1, tiled=True)
     snapshots = relaid.reshape(relaid.shape[0], relaid.shape[1], -1)
-    gram_matrix = lax.psum(pair_gram(snapshots, snapshots), ("blk", "grp"))
-    gram_matrix = gram_matrix / float(rows_here * groups * columns)
-    r_factor = jnp.linalg.cholesky(gram_matrix).T
+    packed = summed(pair_gram(snapshots, snapshots))
+    if groups > 1:
+        packed = lax.psum(packed, "grp")
+    r_factor = factored(packed, snapshots.shape[1], 1.0 / float(rows_here * groups * columns))
     return (r_factor, active_force)
 
 

time: 419 us -> 187 us (0.45)
  other arithmetic: 132 us -> 3.43 us
  blocking collectives: 95.6 us -> 0 us
  Pallas kernels: 0 us -> 72.4 us
  waiting for transfers between devices: 131 us -> 86 us
  between operations: 18.3 us -> 0.75 us
  matrix products: 20.8 us -> 6.32 us
  starting transfers between devices: 0.05 us -> 7.42 us
  local copies, waits for them, and re-layouts: 17 us -> 10 us
    psum x1 -> x0, waiting for transfers between devices: 131 us -> none  [per_device(): gram_matrix = lax.psum(pair_gram(snapshots, snapshots), ('blk', 'grp'))]
    another operation x22 -> x0, other arithmetic: 124 us -> none  [per_device(): r_factor = jnp.linalg.cholesky(gram_matrix).T]
    all_to_all x1 -> x0, blocking collectives: 95.6 us -> none  [per_device(): lax.all_to_all(weighted, 'blk', split_axis=2, concat_axis=1, tiled=True)]
    all_to_all x0 -> x1, waiting for transfers between devices: none -> 86 us  [per_device(): lax.all_to_all(weighted, 'blk', split_axis=2, concat_axis=1, tiled=True)]
    pallas_call x0 -> x2, Pallas kernels: none -> 72.4 us  [the longest x1 37.2 us: summed(): pl.pallas_call(functools.partial(sum_kernel, count), out_shape=jax.ShapeD...]
    another operation x10 -> x0, matrix products: 9.81 us -> none  [per_device(): r_factor = jnp.linalg.cholesky(gram_matrix).T]
    all_to_all x0 -> x1, starting transfers between devices: none -> 7.41 us  [per_device(): lax.all_to_all(weighted, 'blk', split_axis=2, concat_axis=1, tiled=True)]
    unnamed x13 -> x8, local copies, waits for them, and re-layouts: 12.1 us -> 6.5 us
  transfers between devices with their start and end apart: 3 -> 3, of which waited for: 1 -> 1; matrix products, arithmetic and copies ran while one was open for 1% -> 2% of each run, Pallas kernels for 0% -> 0%
where the time goes in v1:
time: 187 us; the launch traced here: 186 us
  waiting for transfers between devices  86 us (46%)
  Pallas kernels  72.4 us (39%)
  local copies, waits for them, and re-layouts  10 us (5%)
  starting transfers between devices  7.42 us (4%)
  matrix products  6.32 us (3%)
  other arithmetic  3.43 us (2%)
    all_to_all x1, waiting for transfers between devices, per_device(): lax.all_to_all(weighted, 'blk', split_axis=2, concat_axis=1, tiled=True)  86 us
    pallas_call x1, Pallas kernels, summed(): pl.pallas_call(functools.partial(sum_kernel, count), out_shape=jax.ShapeD...  37.2 us
    pallas_call x1, Pallas kernels, factored(): pl.pallas_call(functools.partial(chol_kernel, scale), out_shape=jax.Shape...  35.2 us
    all_to_all x1, starting transfers between devices, per_device(): lax.all_to_all(weighted, 'blk', split_axis=2, concat_axis=1, tiled=True)  7.41 us
    unnamed x8, local copies, waits for them, and re-layouts  6.5 us
    dot_general x1, matrix products, pair_gram(): jnp.einsum('ftm,fsm->ts', left_block, right_block, precision=lax.Precisio...  6.32 us
  transfers between devices with their start and end apart: 3, of which 1 were waited for; matrix products, arithmetic and copies ran while one was open for 2% of the time, Pallas kernels for 0%

profile of v1, /device:TPU:0, one launch (start us, length us, event | category | flops | bytes accessed | tf_op | source)
XLA Modules:
  0.0 186.4 jit_solution(9534752936618331942)
XLA Ops:
  0.6 3.0 %copy.12 = f32[3,24,32,256]{3,1,0,2:T(8,128)S(1)} copy(f32[3,24,32,256]{3,2,1,0:T(8,128)} %param.2) | data formatting | bytes 4718592 | tf_op args[0]
  3.7 0.0 collective-permute-start.1
  3.7 0.0 collective-permute-start
  3.7 0.3 fusion.4
  4.0 0.6 fusion.5
  4.5 0.7 fusion.2
  5.2 0.0 copy-start.2
  5.2 0.2 slice.64
  5.5 0.5 copy-done.2
  6.0 0.0 collective-permute-done.1
  6.0 0.0 collective-permute-done
  6.0 0.2 fusion.1
  6.2 0.2 slice_add_fusion
  6.4 0.0 copy-start
  6.4 0.9 copy-done
  7.3 2.3 %maximum_multiply_fusion = f32[5,24,32,256]{3,1,0,2:T(8,128)} fusion(f32[1,24,32,256]{3,1,0,2:T(8,128)S(1)} %get-tuple-element.5, f32[1,24,32,256]{3,1,0,2:T(8,128)S(1)} %get-tuple-element.4, f32[3,24,32,256]{3,1,0,2:T(8,128)S(1)} %copy.12, f32[32,256]{1,0:T(8,128)S(1)} %convert_element_type.3), kind=kLoop, calls=%fused_computation | loop fusion | flops 2949120 | bytes 7897088 | tf_op jit(solution)/shard_map/mul | solution.py:218
  9.5 7.4 %all-to-all-start = ((f32[5,24,32,256]{3,1,0,2:T(8,128)}), f32[5,24,32,256]{3,1,0,2:T(8,128)}, u32[]{:S(2)}, u32[]{:S(2)}) async-start(f32[5,24,32,256]{3,1,0,2:T(8,128)} %maximum_multiply_fusion), calls=%async_computation | async-start | bytes 7864320 | tf_op jit(solution)/shard_map/all_to_all | solution.py:219
  16.9 0.1 pad_maximum_fusion.2
  17.1 2.1 %copy.14 = f32[2,24,32,256]{3,2,1,0:T(8,128)} copy(f32[2,24,32,256]{3,1,0,2:T(8,128)S(1)} %pad_maximum_fusion.2) | data formatting | bytes 3145728
  19.1 86.0 %all-to-all-done = f32[5,24,32,256]{3,1,0,2:T(8,128)} async-done(((f32[5,24,32,256]{3,1,0,2:T(8,128)}), f32[5,24,32,256]{3,1,0,2:T(8,128)}, u32[]{:S(2)}, u32[]{:S(2)}) %all-to-all-start) | async-done | bytes 3932192 | tf_op jit(solution)/shard_map/all_to_all | solution.py:219
  105.2 2.5 %copy.13 = f32[5,32,24,1,256]{4,2,1,0,3:T(8,128)S(1)} copy(f32[5,32,24,1,256]{4,2,0,1,3:T(8,128)} %bitcast.1) | data formatting | bytes 7864320 | tf_op jit(solution)/shard_map/all_to_all | solution.py:219
  107.7 6.3 %convolution_bitcast_fusion.g_ref = f32[768,768]{1,0:T(8,128)} fusion(f32[5,768,256]{2,1,0:T(8,128)S(1)} %bitcast.8), kind=kOutput, calls=%fused_computation.1 | convolution fusion | flops 4529848320 | bytes 6291456 | tf_op jit(solution)/shard_map/ftm,fsm->ts/dot_general | solution.py:206
  114.0 37.2 %shard_map.41.g_ref = f32[2816,128]{1,0:T(8,128)} custom-call(f32[768,768]{1,0:T(8,128)} %convolution_bitcast_fusion.g_ref), custom_call_target="tpu_custom_call" | custom-call | tf_op jit(solution)/shard_map/pallas_call | solution.py:106
  151.2 35.2 %shard_map.42 = f32[768,768]{1,0:T(8,128)} custom-call(f32[2816,128]{1,0:T(8,128)} %shard_map.41.g_ref), custom_call_target="tpu_custom_call" | custom-call | tf_op jit(solution)/shard_map/pallas_call | solution.py:179
  (4 shorter events, 0.0 us)
Async XLA Ops:
  3.7 2.3 %collective-permute-start.1 = (f32[2,24,1,256]{3,1,0,2:T(8,128)S(1)}, f32[2,24,1,256]{3,1,0,2:T(8,128)S(1)}, u32[]{:S(2)}, u32[]{:S(2)}) collective-permute-start(f32[2,24,1,256]{3,1,0,2:T(8,128)S(1)} %get-tuple-element.7), channel_id=1, source_target_pairs={{0,0},{1,1},{2,2},{3,3},{4,4},{5,5},{6,6},{7,7},{8,8},{9,9},{10,10... | collective-permute-start | bytes 147464 | tf_op jit(solution)/shard_map/ppermute | solution.py:196
  3.7 2.3 %collective-permute-start = (f32[2,24,1,256]{3,1,0,2:T(8,128)S(1)}, f32[2,24,1,256]{3,1,0,2:T(8,128)S(1)}, u32[]{:S(2)}, u32[]{:S(2)}) collective-permute-start(f32[2,24,1,256]{3,1,0,2:T(8,128)S(1)} %get-tuple-element.6), channel_id=1, source_target_pairs={{0,0},{1,1},{2,2},{3,3},{4,4},{5,5},{6,6},{7,7},{8,8},{9,9},{10,10... | collective-permute-start | bytes 147464 | tf_op jit(solution)/shard_map/ppermute | solution.py:198
  5.2 0.8 copy-start.2
  6.4 0.9 copy-start
  9.5 7.4 %copy-start.1 = (f32[1,24,32,256]{3,1,0,2:T(8,128)S(1)}, f32[1,24,32,256]{3,1,0,2:T(8,128)}, u32[]{:S(2)}) copy-start(f32[1,24,32,256]{3,1,0,2:T(8,128)} %copy-done) | copy-start | bytes 2359300
  9.5 95.7 %all-to-all-start = ((f32[5,24,32,256]{3,1,0,2:T(8,128)}), f32[5,24,32,256]{3,1,0,2:T(8,128)}, u32[]{:S(2)}, u32[]{:S(2)}) async-start(f32[5,24,32,256]{3,1,0,2:T(8,128)} %maximum_multiply_fusion), calls=%async_computation | async-start | bytes 7864320 | tf_op jit(solution)/shard_map/all_to_all | solution.py:219

commit v2 on v1

--- a/solution.py
+++ b/solution.py
@@ -186,6 +186,116 @@
     )(packed)
 
 
+def pack_kernel(fluid, start_ref, place_ref, x_ref, o_ref):
+    rows, height, columns = x_ref.shape
+    times = o_ref.shape[0]
+    width = columns + NB
+    o_ref[...] = jnp.zeros_like(o_ref)
+    target = lax.broadcasted_iota(jnp.int32, (width, columns), 0)
+
+    @pl.loop(0, rows)
+    def _(row):
+        x = x_ref[row]
+        high = x.astype(jnp.bfloat16).astype(jnp.float32)
+        rest = x - high
+        middle = rest.astype(jnp.bfloat16).astype(jnp.float32)
+        terms = jnp.concatenate([high, middle, rest - middle], 0).astype(jnp.bfloat16)
+        choice = jnp.where(place_ref[pl.ds(row, 1), :] == target, 1.0, 0.0).astype(jnp.bfloat16)
+        moved = lax.dot_general(terms, choice, (((1,), (1,)), ((), ())), preferred_element_type=jnp.float32)
+        moved = moved[:height] + moved[height:2 * height] + moved[2 * height:]
+        for part in range(height // times):
+            span = pl.ds(pl.multiple_of(part * fluid + start_ref[row] * NB, NB), width)
+            o_ref[:, span] += moved[part * times:(part + 1) * times]
+
+
+def packed_points(stacked, mask):
+    quantities, times, rows, columns = stacked.shape
+    fluid = columns * (rows + 2) // 2
+    order = jnp.arange(columns)
+    before = (order[:, None] < order[None, :]).astype(jnp.bfloat16)
+    in_row = jnp.dot(mask.astype(jnp.bfloat16), before, preferred_element_type=jnp.float32).astype(jnp.int32)
+    filled = jnp.sum(mask, 1)
+    ranks = jnp.arange(rows)
+    offset = jnp.sum(jnp.where(ranks[None, :] < ranks[:, None], filled[None, :], 0), 1)
+    place = jnp.where(mask > 0, in_row + (offset % NB)[:, None], -1)
+    by_row = jnp.transpose(stacked, (2, 0, 1, 3)).reshape(rows, quantities * times, columns)
+    return pl.pallas_call(
+        functools.partial(pack_kernel, fluid),
+        out_shape=jax.ShapeDtypeStruct((times, quantities * fluid + columns + NB), jnp.float32),
+        in_specs=[pl.BlockSpec(memory_space=pltpu.SMEM), pl.BlockSpec(memory_space=pltpu.VMEM), pl.BlockSpec(memory_space=pltpu.VMEM)],
+        out_specs=pl.BlockSpec(memory_space=pltpu.VMEM),
+        compiler_params=pltpu.CompilerParams(vmem_limit_bytes=56 * 2**20),
+    )(offset // NB, place, by_row), quantities * fluid // NB
+
+
+def first_chunk(device, chunks, count):
+    return device * chunks // count
+
+
+def exchange_kernel(count, chunks, x_ref, o_ref, send, recv):
+    me = lax.axis_index("blk")
+    times = x_ref.shape[0]
+    least = chunks // count
+    most = -(-chunks // count)
+
+    barrier = pltpu.get_barrier_semaphore()
+
+    def greet(step, carry):
+        pl.semaphore_signal(barrier, inc=1, device_id={"blk": (me + step) % count}, device_id_type=MESH_ID)
+        return carry
+
+    lax.fori_loop(1, count, greet, 0)
+    mine = pl.ds(pl.multiple_of(me * times, 8), times)
+    o_ref[mine, :] = x_ref[:, pl.ds(pl.multiple_of(first_chunk(me, chunks, count) * NB, NB), most * NB)]
+    pl.semaphore_wait(barrier, count - 1)
+
+    def copy(step, number):
+        device = (me + step) % count
+        first = first_chunk(device, chunks, count)
+        return pltpu.make_async_remote_copy(
+            src_ref=x_ref.at[:, pl.ds(pl.multiple_of(first * NB, NB), number * NB)],
+            dst_ref=o_ref.at[mine, pl.ds(0, number * NB)],
+            send_sem=send.at[step - 1], recv_sem=recv.at[step - 1],
+            device_id={"blk": device}, device_id_type=MESH_ID)
+
+    def held(device):
+        return first_chunk(device + 1, chunks, count) - first_chunk(device, chunks, count)
+
+    def each(step, device, act):
+        for number in sorted({least, most}):
+            @pl.when(held(device) == number)
+            def _(number=number):
+                act(copy(step, number))
+
+    def begin(step, carry):
+        each(step, (me + step) % count, lambda c: c.start())
+        return carry
+
+    def finish(step, carry):
+        each(step, me, lambda c: c.wait_recv())
+        each(step, (me + step) % count, lambda c: c.wait_send())
+        return carry
+
+    lax.fori_loop(1, count, begin, 0)
+    lax.fori_loop(1, count, finish, 0)
+
+
+def exchanged(points, chunks):
+    count = lax.axis_size("blk")
+    width = -(-chunks // count) * NB
+    got = pl.pallas_call(
+        functools.partial(exchange_kernel, count, chunks),
+        out_shape=jax.ShapeDtypeStruct((points.shape[0] * count, width), jnp.float32),
+        in_specs=[pl.BlockSpec(memory_space=pltpu.VMEM)],
+        out_specs=pl.BlockSpec(memory_space=pltpu.VMEM),
+        scratch_shapes=[pltpu.SemaphoreType.DMA((count - 1,))] * 2,
+        compiler_params=pltpu.CompilerParams(collective_id=1, has_side_effects=True, vmem_limit_bytes=56 * 2**20),
+    )(points)
+    me = lax.axis_index("blk")
+    valid = (first_chunk(me + 1, chunks, count) - first_chunk(me, chunks, count)) * NB
+    return jnp.where(jnp.arange(width)[None, :] < valid, got, 0.0)
+
+
 def padded(cells, sides, width):
     for axis, dim in sides:
         count = lax.axis_size(axis)
@@ -203,7 +313,7 @@
 
 
 def pair_gram(left_block, right_block):
-    return jnp.einsum("ftm,fsm->ts", left_block, right_block, precision=lax.Precision.HIGH)
+    return jnp.einsum("tm,sm->ts", left_block, right_block, precision=lax.Precision.HIGH)
 
 
 def per_device(fields, mask):
@@ -215,13 +325,11 @@
     stacked = jnp.concatenate([fields, active_force], 0)
     groups = lax.axis_size("grp")
     rows_here, columns = mask.shape
-    weighted = stacked * mask.astype(jnp.float32)[None, None]
-    relaid = lax.all_to_all(weighted, "blk", split_axis=2, concat_axis=1, tiled=True)
-    snapshots = relaid.reshape(relaid.shape[0], relaid.shape[1], -1)
+    snapshots = exchanged(*packed_points(stacked, mask))
     packed = summed(pair_gram(snapshots, snapshots))
     if groups > 1:
         packed = lax.psum(packed, "grp")
-    r_factor = factored(packed, snapshots.shape[1], 1.0 / float(rows_here * groups * columns))
+    r_factor = factored(packed, snapshots.shape[0], 1.0 / float(rows_here * groups * columns))
     return (r_factor, active_force)
 
 

time: 187 us -> 171 us (0.914)
  waiting for transfers between devices: 86 us -> 0.01 us
  Pallas kernels: 72.4 us -> 144 us
  starting transfers between devices: 7.42 us -> 0.01 us
  other arithmetic: 3.43 us -> 5.98 us
  local copies, waits for them, and re-layouts: 10 us -> 12.2 us
    all_to_all x1 -> x0, waiting for transfers between devices: 86 us -> none  [per_device(): lax.all_to_all(weighted, 'blk', split_axis=2, concat_axis=1, tiled=True)]
    pallas_call x0 -> x2, Pallas kernels: none -> 60.8 us  [the longest x1 47.7 us: exchanged(): pl.pallas_call(functools.partial(exchange_kernel, count, chunks), out_sha...]
    pallas_call x1, Pallas kernels: 37.2 us -> 48.2 us  [summed(): pl.pallas_call(functools.partial(sum_kernel, count), out_shape=jax.ShapeD...]
    all_to_all x1 -> x0, starting transfers between devices: 7.41 us -> none  [per_device(): lax.all_to_all(weighted, 'blk', split_axis=2, concat_axis=1, tiled=True)]
    unnamed x8 -> x4, local copies, waits for them, and re-layouts: 6.5 us -> 0.01 us
    slice x2, local copies, waits for them, and re-layouts: 0.82 us -> 5.46 us  [per_device(): slope_cols = 0.5 * (jnp.roll(middle, -1, 3) - jnp.roll(middle, 1, 3))]
    transpose x0 -> x1, local copies, waits for them, and re-layouts: none -> 4.14 us  [packed_points(): jnp.transpose(stacked, (2, 0, 1, 3))]
    all_to_all x1 -> x0, local copies, waits for them, and re-layouts: 2.49 us -> none  [per_device(): lax.all_to_all(weighted, 'blk', split_axis=2, concat_axis=1, tiled=True)]
  transfers between devices with their start and end apart: 3 -> 2, of which waited for: 1 -> 0; matrix products, arithmetic and copies ran while one was open for 2% -> 6% of each run, Pallas kernels for 0% -> 0%
where the time goes in v2:
time: 171 us
  Pallas kernels  144 us (84%)
  local copies, waits for them, and re-layouts  12.2 us (7%)
  matrix products  7.58 us (4%)
  other arithmetic  5.98 us (3%)
    pallas_call x1, Pallas kernels, summed(): pl.pallas_call(functools.partial(sum_kernel, count), out_shape=jax.ShapeD...  48.2 us
    pallas_call x1, Pallas kernels, exchanged(): pl.pallas_call(functools.partial(exchange_kernel, count, chunks), out_sha...  47.7 us
    pallas_call x1, Pallas kernels, factored(): pl.pallas_call(functools.partial(chol_kernel, scale), out_shape=jax.Shape...  35 us
    pallas_call x1, Pallas kernels, packed_points(): pl.pallas_call(functools.partial(pack_kernel, fluid), out_shape=jax.Shape...  13 us
    dot_general x1, matrix products, pair_gram(): jnp.einsum('tm,sm->ts', left_block, right_block, precision=lax.Precision....  6.82 us
    slice x2, local copies, waits for them, and re-layouts, per_device(): slope_cols = 0.5 * (jnp.roll(middle, -1, 3) - jnp.roll(middle, 1, 3))  5.46 us
    transpose x1, local copies, waits for them, and re-layouts, packed_points(): jnp.transpose(stacked, (2, 0, 1, 3))  4.14 us
  transfers between devices with their start and end apart: 2, of which 0 were waited for; matrix products, arithmetic and copies ran while one was open for 6% of the time, Pallas kernels for 0%

profile of v2, /device:TPU:0, one launch (start us, length us, event | category | flops | bytes accessed | tf_op | source)
XLA Modules:
  0.0 170.5 jit_solution(15408553339009919251)
XLA Ops:
  0.6 1.2 fusion.12
  1.8 0.0 collective-permute-start
  1.8 0.0 collective-permute-start.1
  1.9 0.0 copy-start
  1.9 4.3 %fusion.14 = (f32[2,24,32,255]{3,2,1,0:T(8,128)}, f32[2,24,32,255]{3,2,1,0:T(8,128)}) fusion(f32[3,24,32,256]{3,2,1,0:T(8,128)} %param.2), kind=kLoop, calls=%fused_computation.31 | loop fusion | bytes 6266880 | tf_op jit(solution)/shard_map/jit(_roll_static)/slice | solution.py:323
  6.2 1.2 fusion.13
  7.3 0.1 reduce_sum.18
  7.4 0.1 select_reduce_fusion
  7.6 0.6 and_select_fusion
  8.2 0.8 fusion.9.place_ref
  8.9 2.8 %fusion.4 = f32[2,24,32,256]{3,2,1,0:T(8,128)S(1)} fusion(f32[2,24,32,1]{3,2,1,0:T(8,128)} %get-tuple-element.7, f32[2,24,32,255]{3,2,1,0:T(8,128)} %get-tuple-element.9, f32[2,24,32,255]{3,2,1,0:T(8,128)} %get-tuple-element.8, f32[2,24,32,1]{3,2,1,0:T(8,128)S(1)} %get-tuple-element.6), kind=kLoop, calls=%fused_computation.8 | loop fusion | flops 1572864 | bytes 4718592 | tf_op jit(solution)/shard_map/mul | solution.py:323
  11.8 0.0 slice-start
  11.8 0.0 collective-permute-done
  11.8 1.4 slice-done
  13.2 0.4 fusion.3
  13.6 0.3 slice_add_fusion
  13.9 0.4 maximum_bitcast_fusion
  14.3 1.2 pad_maximum_fusion.2
  15.5 4.1 %copy.5 = f32[32,5,24,256]{3,2,1,0:T(8,128)} copy(f32[32,5,24,256]{3,0,2,1:T(8,128)S(1)} %maximum_bitcast_fusion) | data formatting | bytes 7864320 | tf_op jit(solution)/shard_map/transpose | solution.py:221
  19.7 13.0 %shard_map.41.x_ref = f32[24,22144]{1,0:T(8,128)} custom-call(s32[32]{0:T(128)} %get-tuple-element.11.start_ref, s32[32,256]{1,0:T(8,128)} %fusion.9.place_ref, f32[32,120,256]{2,1,0:T(8,128)} %bitcast.7), custom_call_target="tpu_custom_call" | custom-call | tf_op jit(solution)/shard_map/pallas_call | solution.py:222
  32.7 47.7 %shard_map.42 = f32[768,768]{1,0:T(8,128)} custom-call(f32[24,22144]{1,0:T(8,128)} %shard_map.41.x_ref), custom_call_target="tpu_custom_call" | custom-call | tf_op jit(solution)/shard_map/pallas_call | solution.py:286
  80.4 6.8 %fusion.g_ref = f32[768,768]{1,0:T(8,128)} fusion(f32[768,768]{1,0:T(8,128)} %shard_map.42, pred[768]{0:T(1024)(128)(4,1)S(1)} %iota_compare_fusion.3), kind=kOutput, calls=%fused_computation.1 | convolution fusion | flops 2718498816 | bytes 4719360 | tf_op jit(solution)/shard_map/tm,sm->ts/dot_general | solution.py:316
  87.3 48.2 %shard_map.43.g_ref = f32[2816,128]{1,0:T(8,128)} custom-call(f32[768,768]{1,0:T(8,128)} %fusion.g_ref), custom_call_target="tpu_custom_call" | custom-call | tf_op jit(solution)/shard_map/pallas_call | solution.py:106
  135.5 35.0 %shard_map.44 = f32[768,768]{1,0:T(8,128)} custom-call(f32[2816,128]{1,0:T(8,128)} %shard_map.43.g_ref), custom_call_target="tpu_custom_call" | custom-call | tf_op jit(solution)/shard_map/pallas_call | solution.py:179
  (5 shorter events, 0.0 us)
Async XLA Ops:
  1.8 9.9 %collective-permute-start = (f32[2,24,1,256]{3,2,1,0:T(1,128)S(1)}, f32[2,24,1,256]{3,2,1,0:T(1,128)S(1)}, u32[]{:S(2)}, u32[]{:S(2)}) collective-permute-start(f32[2,24,1,256]{3,2,1,0:T(1,128)S(1)} %get-tuple-element.4), channel_id=1, source_target_pairs={{0,0},{1,1},{2,2},{3,3},{4,4},{5,5},{6,6},{7,7},{8,8},{9,9},{10,10... | collective-permute-start | bytes 147464 | tf_op jit(solution)/shard_map/ppermute | solution.py:308
  1.8 9.9 %collective-permute-start.1 = (f32[2,24,1,256]{3,2,1,0:T(1,128)S(1)}, f32[2,24,1,256]{3,2,1,0:T(1,128)S(1)}, u32[]{:S(2)}, u32[]{:S(2)}) collective-permute-start(f32[2,24,1,256]{3,2,1,0:T(1,128)S(1)} %get-tuple-element.5), channel_id=1, source_target_pairs={{0,0},{1,1},{2,2},{3,3},{4,4},{5,5},{6,6},{7,7},{8,8},{9,9},{10,10... | collective-permute-start | bytes 147464 | tf_op jit(solution)/shard_map/ppermute | solution.py:306
  1.9 4.3 %copy-start = (f32[3,24,32,256]{3,2,1,0:T(8,128)S(1)}, f32[3,24,32,256]{3,2,1,0:T(8,128)}, u32[]{:S(2)}) copy-start(f32[3,24,32,256]{3,2,1,0:T(8,128)} %param.2) | copy-start | bytes 7077892
  6.2 1.2 copy-start.1
  11.8 1.4 slice-start

commit v3 on v2

--- a/solution.py
+++ b/solution.py
@@ -41,17 +41,12 @@
         for step in range(1, size):
             pl.semaphore_signal(barrier, inc=1, device_id={"blk": peer(stride, size, step)[1]}, device_id_type=MESH_ID)
             greeted += 1
-    for b, (i, j) in enumerate(tiles(g_ref.shape[0])):
-        acc[b * NB:(b + 1) * NB, :] = g_ref[i * NB:(i + 1) * NB, j * NB:(j + 1) * NB]
-    used = len(tiles(g_ref.shape[0])) * NB
-    total = acc.shape[0]
-    if used < total:
-        acc[used:, :] = jnp.zeros((total - used, NB), jnp.float32)
     pl.semaphore_wait(barrier, greeted)
 
     started = []
     base = 0
-    length = total
+    length = g_ref.shape[0]
+    source = g_ref
     slot = 0
     owned = []
     for (stride, size), buf in zip(plan, bufs):
@@ -61,7 +56,7 @@
         for step in range(1, size):
             there, device = peer(stride, size, step)
             copy = pltpu.make_async_remote_copy(
-                src_ref=acc.at[pl.ds(pl.multiple_of(base + there * length, 8), length)],
+                src_ref=source.at[pl.ds(pl.multiple_of(base + there * length, 8), length)],
                 dst_ref=buf.at[step - 1],
                 send_sem=send.at[slot], recv_sem=recv.at[slot],
                 device_id={"blk": device}, device_id_type=MESH_ID)
@@ -69,11 +64,12 @@
             wave.append(copy)
             slot += 1
         base = pl.multiple_of(base + here * length, 8)
-        value = acc[pl.ds(base, length), :]
+        value = source[pl.ds(base, length), :]
         for step, copy in enumerate(wave):
             copy.wait_recv()
             value = value + buf[step]
         acc[pl.ds(base, length), :] = value
+        source = acc
         owned.append((base, length))
         started += wave
     full[pl.ds(base, length), :] = acc[pl.ds(base, length), :]
@@ -98,8 +94,7 @@
 
 def summed(gram):
     count = lax.axis_size("blk")
-    size = gram.shape[0]
-    total = packed_rows(size, count)
+    total = gram.shape[0]
     plan = stages(count)
     lengths = [total // 2, total // 8, total // count]
     copies = sum(s - 1 for _, s in plan)
@@ -186,46 +181,80 @@
     )(packed)
 
 
-def pack_kernel(fluid, start_ref, place_ref, x_ref, o_ref):
-    rows, height, columns = x_ref.shape
+def pack_kernel(fluid, x_ref, above_ref, below_ref, mask_ref, o_ref, force_ref, rank_ref, *halves):
+    rows, columns = mask_ref.shape
     times = o_ref.shape[0]
     width = columns + NB
     o_ref[...] = jnp.zeros_like(o_ref)
+    cells, forces = halves[:columns // NB], halves[columns // NB:]
+    for h, half in enumerate(cells):
+        half[...] = x_ref[:, h * NB:(h + 1) * NB]
     target = lax.broadcasted_iota(jnp.int32, (width, columns), 0)
-
-    @pl.loop(0, rows)
-    def _(row):
-        x = x_ref[row]
+    before = lax.broadcasted_iota(jnp.int32, (columns, columns), 0) < lax.broadcasted_iota(jnp.int32, (columns, columns), 1)
+    ones = jnp.where(mask_ref[...] > 0, 1.0, 0.0)
+    rank_ref[...] = jnp.dot(
+        ones.astype(jnp.bfloat16), jnp.where(before, 1.0, 0.0).astype(jnp.bfloat16), preferred_element_type=jnp.float32
+    ).astype(jnp.int32)
+
+    def load(quantity, row):
+        span = pl.ds(quantity * times * rows + row, times, stride=rows)
+        return jnp.concatenate([half[span, :] for half in cells], 1)
+
+    def side_slope(values):
+        return 0.5 * (pltpu.roll(values, columns - 1, 1) - pltpu.roll(values, 1, 1))
+
+    def step(row, filled):
+        slopes = []
+        here = [load(quantity, row) for quantity in range(3)]
+        for q in range(2):
+            span = slice(q * times, (q + 1) * times)
+            upper = jnp.where(row == 0, above_ref[span, :], load(q + 1, jnp.maximum(row - 1, 0)))
+            lower = jnp.where(row == rows - 1, below_ref[span, :], load(q + 1, jnp.minimum(row + 1, rows - 1)))
+            slopes.append(0.5 * (lower - upper))
+        force_x = slopes[0] + side_slope(here[2])
+        force_y = slopes[1] - side_slope(here[1])
+        for h, half in enumerate(forces):
+            half[pl.ds(row, times, stride=rows), :] = force_x[:, h * NB:(h + 1) * NB]
+            half[pl.ds(times * rows + row, times, stride=rows), :] = force_y[:, h * NB:(h + 1) * NB]
+        x = jnp.concatenate(here + [force_x, force_y], 0)
+        height = 5 * times
         high = x.astype(jnp.bfloat16).astype(jnp.float32)
         rest = x - high
         middle = rest.astype(jnp.bfloat16).astype(jnp.float32)
         terms = jnp.concatenate([high, middle, rest - middle], 0).astype(jnp.bfloat16)
-        choice = jnp.where(place_ref[pl.ds(row, 1), :] == target, 1.0, 0.0).astype(jnp.bfloat16)
+        open_row = mask_ref[pl.ds(row, 1), :] > 0
+        place = jnp.where(open_row, rank_ref[pl.ds(row, 1), :] + lax.rem(filled, NB), -1)
+        choice = jnp.where(place == target, 1.0, 0.0).astype(jnp.bfloat16)
         moved = lax.dot_general(terms, choice, (((1,), (1,)), ((), ())), preferred_element_type=jnp.float32)
         moved = moved[:height] + moved[height:2 * height] + moved[2 * height:]
-        for part in range(height // times):
-            span = pl.ds(pl.multiple_of(part * fluid + start_ref[row] * NB, NB), width)
+        start = lax.div(filled, NB) * NB
+        for part in range(5):
+            span = pl.ds(pl.multiple_of(part * fluid + start, NB), width)
             o_ref[:, span] += moved[part * times:(part + 1) * times]
-
-
-def packed_points(stacked, mask):
-    quantities, times, rows, columns = stacked.shape
+        return filled + jnp.sum(jnp.where(open_row, 1.0, 0.0)).astype(jnp.int32)
+
+    lax.fori_loop(0, rows, step, jnp.int32(0))
+    for h, half in enumerate(forces):
+        force_ref[:, h * NB:(h + 1) * NB] = half[...]
+
+
+def packed_points(fields, above, below, mask):
+    quantities, times, rows, columns = fields.shape
     fluid = columns * (rows + 2) // 2
-    order = jnp.arange(columns)
-    before = (order[:, None] < order[None, :]).astype(jnp.bfloat16)
-    in_row = jnp.dot(mask.astype(jnp.bfloat16), before, preferred_element_type=jnp.float32).astype(jnp.int32)
-    filled = jnp.sum(mask, 1)
-    ranks = jnp.arange(rows)
-    offset = jnp.sum(jnp.where(ranks[None, :] < ranks[:, None], filled[None, :], 0), 1)
-    place = jnp.where(mask > 0, in_row + (offset % NB)[:, None], -1)
-    by_row = jnp.transpose(stacked, (2, 0, 1, 3)).reshape(rows, quantities * times, columns)
-    return pl.pallas_call(
+    points, force = pl.pallas_call(
         functools.partial(pack_kernel, fluid),
-        out_shape=jax.ShapeDtypeStruct((times, quantities * fluid + columns + NB), jnp.float32),
-        in_specs=[pl.BlockSpec(memory_space=pltpu.SMEM), pl.BlockSpec(memory_space=pltpu.VMEM), pl.BlockSpec(memory_space=pltpu.VMEM)],
-        out_specs=pl.BlockSpec(memory_space=pltpu.VMEM),
+        out_shape=(
+            jax.ShapeDtypeStruct((times, 5 * fluid + columns + NB), jnp.float32),
+            jax.ShapeDtypeStruct((2 * times * rows, columns), jnp.float32),
+        ),
+        in_specs=[pl.BlockSpec(memory_space=pltpu.VMEM)] * 4,
+        out_specs=(pl.BlockSpec(memory_space=pltpu.VMEM),) * 2,
+        scratch_shapes=[pltpu.VMEM((rows, columns), jnp.int32)]
+        + [pltpu.VMEM((3 * times * rows, NB), jnp.float32)] * (columns // NB)
+        + [pltpu.VMEM((2 * times * rows, NB), jnp.float32)] * (columns // NB),
         compiler_params=pltpu.CompilerParams(vmem_limit_bytes=56 * 2**20),
-    )(offset // NB, place, by_row), quantities * fluid // NB
+    )(fields.reshape(-1, columns), above.reshape(-1, columns), below.reshape(-1, columns), mask)
+    return points, 5 * fluid // NB, force.reshape(2, times, rows, columns)
 
 
 def first_chunk(device, chunks, count):
@@ -283,7 +312,7 @@
 def exchanged(points, chunks):
     count = lax.axis_size("blk")
     width = -(-chunks // count) * NB
-    got = pl.pallas_call(
+    return pl.pallas_call(
         functools.partial(exchange_kernel, count, chunks),
         out_shape=jax.ShapeDtypeStruct((points.shape[0] * count, width), jnp.float32),
         in_specs=[pl.BlockSpec(memory_space=pltpu.VMEM)],
@@ -291,45 +320,66 @@
         scratch_shapes=[pltpu.SemaphoreType.DMA((count - 1,))] * 2,
         compiler_params=pltpu.CompilerParams(collective_id=1, has_side_effects=True, vmem_limit_bytes=56 * 2**20),
     )(points)
+
+
+def gram_kernel(count, chunks, x_ref, g_ref, high_ref, low_ref):
+    size, width = x_ref.shape
     me = lax.axis_index("blk")
     valid = (first_chunk(me + 1, chunks, count) - first_chunk(me, chunks, count)) * NB
-    return jnp.where(jnp.arange(width)[None, :] < valid, got, 0.0)
-
-
-def padded(cells, sides, width):
-    for axis, dim in sides:
-        count = lax.axis_size(axis)
-        head = lax.slice_in_dim(cells, 0, width, axis=dim)
-        tail = lax.slice_in_dim(cells, cells.shape[dim] - width, cells.shape[dim], axis=dim)
-        cells = jnp.concatenate(
-            [
-                lax.ppermute(tail, axis, [(i, (i + 1) % count) for i in range(count)]),
-                cells,
-                lax.ppermute(head, axis, [((i + 1) % count, i) for i in range(count)]),
-            ],
-            axis=dim,
-        )
-    return cells
-
-
-def pair_gram(left_block, right_block):
-    return jnp.einsum("tm,sm->ts", left_block, right_block, precision=lax.Precision.HIGH)
+    x = jnp.where(lax.broadcasted_iota(jnp.int32, (size, width), 1) < valid, x_ref[...], 0.0)
+    high_ref[...] = x.astype(jnp.bfloat16)
+    low_ref[...] = (x - x.astype(jnp.bfloat16).astype(jnp.float32)).astype(jnp.bfloat16)
+
+    def times(left, right):
+        return lax.dot_general(left, right, (((1,), (1,)), ((), ())), preferred_element_type=jnp.float32)
+
+    b = 0
+    for i in range(size // NB):
+        rows = slice(i * NB, (i + 1) * NB)
+        strip = times(high_ref[rows, :], high_ref[i * NB:, :])
+        strip = strip + times(high_ref[rows, :], low_ref[i * NB:, :])
+        strip = strip + times(low_ref[rows, :], high_ref[i * NB:, :])
+        for j in range(size // NB - i):
+            g_ref[b * NB:(b + 1) * NB, :] = strip[:, j * NB:(j + 1) * NB]
+            b += 1
+    if b * NB < g_ref.shape[0]:
+        g_ref[b * NB:, :] = jnp.zeros((g_ref.shape[0] - b * NB, NB), jnp.float32)
+
+
+def upper_gram(snapshots, chunks):
+    count = lax.axis_size("blk")
+    return pl.pallas_call(
+        functools.partial(gram_kernel, count, chunks),
+        out_shape=jax.ShapeDtypeStruct((packed_rows(snapshots.shape[0], count), NB), jnp.float32),
+        in_specs=[pl.BlockSpec(memory_space=pltpu.VMEM)],
+        out_specs=pl.BlockSpec(memory_space=pltpu.VMEM),
+        scratch_shapes=[pltpu.VMEM(snapshots.shape, jnp.bfloat16)] * 2,
+        compiler_params=pltpu.CompilerParams(vmem_limit_bytes=56 * 2**20),
+    )(snapshots)
+
+
+def row_edges(cells):
+    count = lax.axis_size("grp")
+    head, tail = cells[:, :, 0], cells[:, :, -1]
+    if count == 1:
+        return tail, head
+    return (
+        lax.ppermute(tail, "grp", [(i, (i + 1) % count) for i in range(count)]),
+        lax.ppermute(head, "grp", [((i + 1) % count, i) for i in range(count)]),
+    )
 
 
 def per_device(fields, mask):
-    widened = padded(fields[1:3], (("grp", 2),), 1)
-    middle = widened[:, :, 1:-1]
-    slope_rows = 0.5 * (widened[:, :, 2:] - widened[:, :, :-2])
-    slope_cols = 0.5 * (jnp.roll(middle, -1, 3) - jnp.roll(middle, 1, 3))
-    active_force = jnp.stack([slope_rows[0] + slope_cols[1], slope_rows[1] - slope_cols[0]])
-    stacked = jnp.concatenate([fields, active_force], 0)
+    above, below = row_edges(fields[1:3])
     groups = lax.axis_size("grp")
     rows_here, columns = mask.shape
-    snapshots = exchanged(*packed_points(stacked, mask))
-    packed = summed(pair_gram(snapshots, snapshots))
+    points, chunks, active_force = packed_points(fields, above, below, mask)
+    snapshots = exchanged(points, chunks)
+    size = snapshots.shape[0]
+    packed = summed(upper_gram(snapshots, chunks))
     if groups > 1:
         packed = lax.psum(packed, "grp")
-    r_factor = factored(packed, snapshots.shape[0], 1.0 / float(rows_here * groups * columns))
+    r_factor = factored(packed, size, 1.0 / float(rows_here * groups * columns))
     return (r_factor, active_force)
 
 

time: 171 us -> 158 us (0.924)
  Pallas kernels: 144 us -> 155 us
  local copies, waits for them, and re-layouts: 12.2 us -> 2.42 us
  matrix products: 7.58 us -> 0 us
  other arithmetic: 5.98 us -> 0 us
    pallas_call x1 -> x2, Pallas kernels: 13 us -> 23.8 us  [the longest x1 17.2 us: packed_points(): pl.pallas_call(functools.partial(pack_kernel, fluid), out_shape=(jax.Shap...]
    dot_general x2 -> x0, matrix products: 7.58 us -> none  [the longest x1 6.82 us: pair_gram(): jnp.einsum('tm,sm->ts', left_block, right_block, precision=lax.Precision....]
    slice x5 -> x1, local copies, waits for them, and re-layouts: 8.03 us -> 1.19 us  [row_edges(): head, tail = (cells[:, :, 0], cells[:, :, -1])]
    transpose x1 -> x0, local copies, waits for them, and re-layouts: 4.14 us -> none  [packed_points(): jnp.transpose(stacked, (2, 0, 1, 3))]
    mul x2 -> x0, other arithmetic: 3.25 us -> none  [the longest x1 2.8 us: per_device(): slope_cols = 0.5 * (jnp.roll(middle, -1, 3) - jnp.roll(middle, 1, 3))]
  transfers between devices with their start and end apart: 2 -> 0, of which waited for: 0 -> 0; matrix products, arithmetic and copies ran while one was open for 6% -> 0% of each run, Pallas kernels for 0% -> 0%
where the time goes in v3:
time: 158 us
  Pallas kernels  155 us (98%)
  local copies, waits for them, and re-layouts  2.42 us (2%)
    pallas_call x1, Pallas kernels, summed(): pl.pallas_call(functools.partial(sum_kernel, count), out_shape=jax.ShapeD...  47.9 us
    pallas_call x1, Pallas kernels, exchanged(): pl.pallas_call(functools.partial(exchange_kernel, count, chunks), out_sha...  47.8 us
    pallas_call x1, Pallas kernels, factored(): pl.pallas_call(functools.partial(chol_kernel, scale), out_shape=jax.Shape...  35 us
    pallas_call x1, Pallas kernels, packed_points(): pl.pallas_call(functools.partial(pack_kernel, fluid), out_shape=(jax.Shap...  17.2 us
    pallas_call x1, Pallas kernels, upper_gram(): pl.pallas_call(functools.partial(gram_kernel, count, chunks), out_shape=j...  6.62 us

profile of v3, /device:TPU:0, one launch (start us, length us, event | category | flops | bytes accessed | tf_op | source)
XLA Modules:
  0.0 157.6 jit_solution(3347046638885766333)
XLA Ops:
  0.6 1.2 fusion
  1.8 0.6 copy.7
  2.4 0.6 copy.6
  3.1 17.2 %shard_map.41 = (f32[24,22144]{1,0:T(8,128)}, f32[1536,256]{1,0:T(8,128)}) custom-call(f32[2304,256]{1,0:T(8,128)} %bitcast.4, f32[48,256]{1,0:T(8,128)} %bitcast.6, f32[48,256]{1,0:T(8,128)} %bitcast.5, s32[32,256]{1,0:T(8,128)} %mask_ref.1), custom_call_target="tpu_custom_call" | custom-call | tf_op jit(solution)/shard_map/pallas_call | solution.py:244
  20.3 47.8 %shard_map.42.x_ref = f32[768,768]{1,0:T(8,128)} custom-call(f32[24,22144]{1,0:T(8,128)} %get-tuple-element.4.x_ref), custom_call_target="tpu_custom_call" | custom-call | tf_op jit(solution)/shard_map/pallas_call | solution.py:315
  68.0 6.6 %shard_map.43.g_ref = f32[2816,128]{1,0:T(8,128)} custom-call(f32[768,768]{1,0:T(8,128)} %shard_map.42.x_ref), custom_call_target="tpu_custom_call" | custom-call | tf_op jit(solution)/shard_map/pallas_call | solution.py:351
  74.7 47.9 %shard_map.44.g_ref = f32[2816,128]{1,0:T(8,128)} custom-call(f32[2816,128]{1,0:T(8,128)} %shard_map.43.g_ref), custom_call_target="tpu_custom_call" | custom-call | tf_op jit(solution)/shard_map/pallas_call | solution.py:101
  122.6 35.0 %shard_map.45 = f32[768,768]{1,0:T(8,128)} custom-call(f32[2816,128]{1,0:T(8,128)} %shard_map.44.g_ref), custom_call_target="tpu_custom_call" | custom-call | tf_op jit(solution)/shard_map/pallas_call | solution.py:174

commit v4 on v3

--- a/solution.py
+++ b/solution.py
@@ -7,6 +7,7 @@
 from jax.sharding import PartitionSpec as P
 
 NB = 128
+PARTS = 2
 HIGHEST = lax.Precision.HIGHEST
 MESH_ID = pl.DeviceIdType.MESH
 
@@ -17,7 +18,7 @@
 
 
 def packed_rows(size, count):
-    unit = 8 * count
+    unit = 8 * count * PARTS
     return -(-len(tiles(size)) * NB // unit) * unit
 
 
@@ -44,50 +45,71 @@
     pl.semaphore_wait(barrier, greeted)
 
     started = []
-    base = 0
-    length = g_ref.shape[0]
-    source = g_ref
-    slot = 0
-    owned = []
-    for (stride, size), buf in zip(plan, bufs):
-        length = length // size
-        here = (me // stride) % size
-        wave = []
+    part = g_ref.shape[0] // PARTS
+    copies = sum(size - 1 for _, size in plan)
+    state = [dict(base=half * part, length=part, source=g_ref, owned=[]) for half in range(PARTS)]
+    slots = [sum(size - 1 for _, size in plan[:k]) for k in range(len(plan))]
+
+    def scatter_begin(half, k):
+        at = state[half]
+        stride, size = plan[k]
+        at["length"] //= size
+        at["wave"] = []
         for step in range(1, size):
             there, device = peer(stride, size, step)
+            slot = half * copies + slots[k] + step - 1
             copy = pltpu.make_async_remote_copy(
-                src_ref=source.at[pl.ds(pl.multiple_of(base + there * length, 8), length)],
-                dst_ref=buf.at[step - 1],
+                src_ref=at["source"].at[pl.ds(pl.multiple_of(at["base"] + there * at["length"], 8), at["length"])],
+                dst_ref=bufs[k].at[half * (size - 1) + step - 1],
                 send_sem=send.at[slot], recv_sem=recv.at[slot],
                 device_id={"blk": device}, device_id_type=MESH_ID)
             copy.start()
-            wave.append(copy)
-            slot += 1
-        base = pl.multiple_of(base + here * length, 8)
-        value = source[pl.ds(base, length), :]
-        for step, copy in enumerate(wave):
+            at["wave"].append(copy)
+
+    def scatter_end(half, k):
+        at = state[half]
+        stride, size = plan[k]
+        at["base"] = pl.multiple_of(at["base"] + ((me // stride) % size) * at["length"], 8)
+        piece = pl.ds(at["base"], at["length"])
+        value = at["source"][piece, :]
+        for step, copy in enumerate(at["wave"]):
             copy.wait_recv()
-            value = value + buf[step]
-        acc[pl.ds(base, length), :] = value
-        source = acc
-        owned.append((base, length))
-        started += wave
-    full[pl.ds(base, length), :] = acc[pl.ds(base, length), :]
-    slot = 0
-    for (stride, size), (base, length) in reversed(list(zip(plan, owned))):
-        piece = pl.ds(base, length)
-        wave = []
+            value = value + bufs[k][half * (size - 1) + step]
+        target = acc if k < len(plan) - 1 else full
+        target[piece, :] = value
+        at["source"] = acc
+        at["owned"].append(piece)
+        started.extend(at["wave"])
+
+    def gather_begin(half, k):
+        at = state[half]
+        stride, size = plan[k]
+        piece = at["owned"][k]
+        at["wave"] = []
         for step in range(1, size):
+            slot = half * copies + slots[k] + step - 1
             copy = pltpu.make_async_remote_copy(
                 src_ref=full.at[piece], dst_ref=full.at[piece],
                 send_sem=gsend.at[slot], recv_sem=grecv.at[slot],
                 device_id={"blk": peer(stride, size, step)[1]}, device_id_type=MESH_ID)
             copy.start()
-            wave.append(copy)
-            slot += 1
-        for copy in wave:
+            at["wave"].append(copy)
+
+    def gather_end(half, k):
+        for copy in state[half]["wave"]:
             copy.wait_recv()
-        started += wave
+        started.extend(state[half]["wave"])
+
+    last = len(plan) - 1
+    todo = [(scatter_begin, scatter_end, k) for k in range(last + 1)]
+    todo += [(gather_begin, gather_end, k) for k in range(last, -1, -1)]
+    for half in range(PARTS):
+        todo[0][0](half, todo[0][2])
+    for now, (_, end, k) in enumerate(todo):
+        for half in range(PARTS):
+            end(half, k)
+            if now + 1 < len(todo):
+                todo[now + 1][0](half, todo[now + 1][2])
     for copy in started:
         copy.wait_send()
 
@@ -96,7 +118,7 @@
     count = lax.axis_size("blk")
     total = gram.shape[0]
     plan = stages(count)
-    lengths = [total // 2, total // 8, total // count]
+    lengths = [total // 2 // PARTS, total // 8 // PARTS, total // count // PARTS]
     copies = sum(s - 1 for _, s in plan)
     return pl.pallas_call(
         functools.partial(sum_kernel, count),
@@ -104,8 +126,8 @@
         in_specs=[pl.BlockSpec(memory_space=pltpu.VMEM)],
         out_specs=pl.BlockSpec(memory_space=pltpu.VMEM),
         scratch_shapes=[pltpu.VMEM((total, NB), jnp.float32)]
-        + [pltpu.VMEM((s - 1, rows, NB), jnp.float32) for (_, s), rows in zip(plan, lengths)]
-        + [pltpu.SemaphoreType.DMA((copies,))] * 4,
+        + [pltpu.VMEM(((s - 1) * PARTS, rows, NB), jnp.float32) for (_, s), rows in zip(plan, lengths)]
+        + [pltpu.SemaphoreType.DMA((copies * PARTS,))] * 4,
         compiler_params=pltpu.CompilerParams(collective_id=0, has_side_effects=True, vmem_limit_bytes=56 * 2**20),
     )(gram)
 

time: 158 us -> 155 us (0.981)
  Pallas kernels: 155 us -> 151 us
    pallas_call x1, Pallas kernels: 47.9 us -> 44.7 us  [summed(): pl.pallas_call(functools.partial(sum_kernel, count), out_shape=jax.ShapeD...]
where the time goes in v4:
time: 155 us; the launch traced here: 154 us
  Pallas kernels  151 us (97%)
  local copies, waits for them, and re-layouts  2.42 us (2%)
    pallas_call x1, Pallas kernels, exchanged(): pl.pallas_call(functools.partial(exchange_kernel, count, chunks), out_sha...  47.8 us
    pallas_call x1, Pallas kernels, summed(): pl.pallas_call(functools.partial(sum_kernel, count), out_shape=jax.ShapeD...  44.7 us
    pallas_call x1, Pallas kernels, factored(): pl.pallas_call(functools.partial(chol_kernel, scale), out_shape=jax.Shape...  35.1 us
    pallas_call x1, Pallas kernels, packed_points(): pl.pallas_call(functools.partial(pack_kernel, fluid), out_shape=(jax.Shap...  17.2 us
    pallas_call x1, Pallas kernels, upper_gram(): pl.pallas_call(functools.partial(gram_kernel, count, chunks), out_shape=j...  6.66 us

profile of v4, /device:TPU:0, one launch (start us, length us, event | category | flops | bytes accessed | tf_op | source)
XLA Modules:
  0.0 154.5 jit_solution(18225418358906952677)
XLA Ops:
  0.6 1.2 fusion
  1.8 0.6 copy.7
  2.4 0.6 copy.6
  3.1 17.2 %shard_map.41 = (f32[24,22144]{1,0:T(8,128)}, f32[1536,256]{1,0:T(8,128)}) custom-call(f32[2304,256]{1,0:T(8,128)} %bitcast.4, f32[48,256]{1,0:T(8,128)} %bitcast.6, f32[48,256]{1,0:T(8,128)} %bitcast.5, s32[32,256]{1,0:T(8,128)} %mask_ref.1), custom_call_target="tpu_custom_call" | custom-call | tf_op jit(solution)/shard_map/pallas_call | solution.py:266
  20.3 47.8 %shard_map.42.x_ref = f32[768,768]{1,0:T(8,128)} custom-call(f32[24,22144]{1,0:T(8,128)} %get-tuple-element.4.x_ref), custom_call_target="tpu_custom_call" | custom-call | tf_op jit(solution)/shard_map/pallas_call | solution.py:337
  68.0 6.7 %shard_map.43.g_ref = f32[3072,128]{1,0:T(8,128)} custom-call(f32[768,768]{1,0:T(8,128)} %shard_map.42.x_ref), custom_call_target="tpu_custom_call" | custom-call | tf_op jit(solution)/shard_map/pallas_call | solution.py:373
  74.7 44.7 %shard_map.44.g_ref = f32[3072,128]{1,0:T(8,128)} custom-call(f32[3072,128]{1,0:T(8,128)} %shard_map.43.g_ref), custom_call_target="tpu_custom_call" | custom-call | tf_op jit(solution)/shard_map/pallas_call | solution.py:123
  119.4 35.1 %shard_map.45 = f32[768,768]{1,0:T(8,128)} custom-call(f32[3072,128]{1,0:T(8,128)} %shard_map.44.g_ref), custom_call_target="tpu_custom_call" | custom-call | tf_op jit(solution)/shard_map/pallas_call | solution.py:196
